TPU v7x, 512 devices: a whole 4x8x8 slice. The times are simulated.
512 devices in a mesh: shot: 32 (over y, z_hi), point: 16 (over z_lo, x, core).
Axes of the slice: x: 4, y: 8, z: 8 (z_hi: 4, z_lo: 2; z = z_hi * 2 + z_lo), core: 2. Of those that a mesh axis runs over, the one named last changes fastest.
Arguments:
- traces: bfloat16 [64, 32, 1024], P('shot', 'point'), may hold values from -6 to 6
- panels: bfloat16 [32, 256, 1024], P('point', 'shot'), may hold values from -0.09375 to 0.09375
- aperture: int32 [64, 32], P('shot', 'point'), may hold values 0 or 1
- window_lo: int32 [256, 64], P('point', 'shot'), may hold values from 0 to 255
- window_hi: int32 [256, 64], P('point', 'shot'), may hold values from 512 to 1023
Outputs:
- multiples: bfloat16 [256, 64, 1024], P('point', 'shot')
All inputs are finite; a program needn't handle non-finite values. No bound on the sum of `aperture` on one device may be relied on, other than what follows from the above.
Results may differ from a plain program's by a relative error of at most 0.001.
Values may be sent and summed in bfloat16 or wider, within the bound.
A program may use at most 64 MiB of HBM per device.

v0:
```python
import jax
import jax.numpy as jnp
from jax import lax
from jax.sharding import PartitionSpec as P


def toeplitz(series):
    count = series.shape[-1]
    padded = jnp.concatenate([series, jnp.zeros_like(series)], -1)
    tiled_flat = jnp.tile(padded, (1, count))[:, : count * (2 * count - 1)]
    return tiled_flat.reshape(series.shape[0], count, 2 * count - 1)[:, :, :count]


def window_weights(window_lo, window_hi, length):
    sample_axis = jnp.arange(length).astype(jnp.float32)[None, None, :]
    lower = window_lo.astype(jnp.float32)[:, :, None]
    upper = window_hi.astype(jnp.float32)[:, :, None]
    rising = jnp.clip((sample_axis - lower + 32.0) / 32.0, 0.0, 1.0)
    falling = jnp.clip((upper - sample_axis) / 32.0, 0.0, 1.0)
    return rising * falling


def body(traces, panels, aperture, window_lo, window_hi):
    masked = traces * aperture[:, :, None].astype(traces.dtype)
    local_points = masked.shape[1]

    def kernel_maker():

        def kernel_for(point):
            return toeplitz(lax.dynamic_index_in_dim(masked, point, 1, keepdims=False))

        return kernel_for

    def make_convolve(kernel_for):

        def convolve(panel_piece, first_row):

            def one_point(point, total_sum):
                panel_rows = lax.dynamic_index_in_dim(panel_piece, point, 0, keepdims=False)
                return total_sum + jnp.einsum(
                    "ru,sut->rst", panel_rows, kernel_for(point), preferred_element_type=jnp.float32
                )

            initial = jnp.zeros(
                (panel_piece.shape[1], masked.shape[0], masked.shape[2]), jnp.float32
            )
            return lax.fori_loop(0, local_points, one_point, initial)

        return convolve

    convolve = make_convolve(kernel_maker())
    partial_terms = convolve(lax.all_gather(panels, "shot", axis=1, tiled=True), jnp.int32(0))
    predicted = lax.psum_scatter(partial_terms, "point", scatter_dimension=0, tiled=True)
    weights = window_weights(window_lo, window_hi, traces.shape[2])
    return (weights * predicted).astype(jnp.bfloat16)


def solution(mesh):
    in_specs = (
        P("shot", "point", None),
        P("point", "shot", None),
        P("shot", "point"),
        P("point", "shot"),
        P("point", "shot"),
    )
    out_specs = P("point", "shot", None)
    return jax.shard_map(body, mesh=mesh, in_specs=in_specs, out_specs=out_specs, check_vma=False)
```

profile of v0, /device:TPU:1, one launch (start us, length us, event | category | flops | bytes accessed | tf_op | source)
XLA Modules:
  0.0 359.0 jit_solution(9905600033228501757)
XLA Ops:
  6.5 0.0 all-gather.2.cloned.1.call-start
  6.5 0.7 all-gather.2.cloned.1.call-update
  7.3 0.0 all-reduce.4.cloned.1.call-start
  7.3 0.7 convert_element_type.25
  8.0 0.1 copy.18
  8.1 0.8 copy_multiply_fusion
  8.9 87.5 %all-gather.2.cloned.1.call-done = bf16[2,256,1024]{2,1,0:T(8,128)(2,1)} async-done(((bf16[2,8,1024]{2,1,0:T(8,128)(2,1)}), bf16[2,256,1024]{2,1,0:T(8,128)(2,1)}) %all-gather.2.cloned.1.call-update) | async-done | bytes 1048592 | tf_op jit(solution)/shard_map/all_gather | solution.py:52
  96.4 117.5 %while.14 = (s32[]{:T(128)}, f32[256,2,1024]{2,0,1:T(8,128)S(1)}, bf16[2,256,1024]{2,1,0:T(8,128)(2,1)}, bf16[2,2,1024]{2,0,1:T(2,128)(2,1)S(1)}, s32[]{:T(128)}, /*index=5*/bf16[]{:T(256)}, s32[]{:T(128)}) while((s32[]{:T(128)}, f32[256,2,1024]{2,0,1:T(8,128)S(1)}, bf16[2,256,1024]{2,1,0:T(8,128)(2,1)}, ...), condition=%wide.region_1.2_spmd.clone, body=%wide.region_0.1_spmd.clone.sunk | while | flops 1074790400 | bytes 88609400 | solution.py:47
  96.4 1.1 broadcast_bitcast_fusion.2
  97.4 17.3 %copy.24 = bf16[1,2,1024,2048]{3,1,2,0:T(2,128)(2,1)S(1)} copy(bf16[1,2,1024,2048]{3,2,1,0:T(8,128)(2,1)S(1)} %broadcast_bitcast_fusion.2) | data formatting | bytes 16777216 | tf_op jit(solution)/shard_map/while
  114.8 7.2 %slice.25 = bf16[2,2096128]{1,0:T(2,128)(2,1)} slice(bf16[2,2097152]{1,0:T(2,128)(2,1)S(1)} %bitcast.18), slice={[0:2], [0:2096128]} | slice | bytes 16769024 | tf_op jit(solution)/shard_map/while/body/eval_jaxpr/slice | solution.py:10
  121.9 11.9 %reshape.26 = bf16[4192256]{0:T(1024)(128)(2,1)} reshape(bf16[2,2096128]{1,0:T(2,128)(2,1)} %slice.25) | data formatting | bytes 16769024 | tf_op jit(solution)/shard_map/while
  133.8 0.0 copy-start.2
  133.8 17.4 %reshape.27 = bf16[2,1024,2047]{2,1,0:T(8,128)(2,1)} reshape(bf16[4192256]{0:T(1024)(128)(2,1)} %reshape.26) | data formatting | bytes 16769024 | tf_op jit(solution)/shard_map/while/body/eval_jaxpr/reshape | solution.py:11
  151.2 0.0 copy-done.2
  151.2 3.9 %select_add_fusion.2 = f32[256,2,1024]{2,0,1:T(8,128)S(1)} fusion(f32[256,2,1024]{2,0,1:T(8,128)S(1)} %get-tuple-element.141, bf16[2,1024,2047]{2,1,0:T(8,128)(2,1)} %reshape.27, pred[]{:T(512)S(6)} %compare.4, bf16[2,256,1024]{2,1,0:T(8,128)(2,1)S(1)} %copy-done.2, s32[]{:T(128)} %get-tuple-element.140), kind=kOutput, calls=%fused_computation.3.clone.1 | convolution fusion | flops 1074790400 | bytes 8913409 | tf_op jit(solution)/shard_map/while/body/eval_jaxpr/ru,sut->rst/dot_general | solution.py:40
  155.2 1.1 broadcast_bitcast_fusion.2
  156.2 17.3 %copy.24 = bf16[1,2,1024,2048]{3,1,2,0:T(2,128)(2,1)S(1)} copy(bf16[1,2,1024,2048]{3,2,1,0:T(8,128)(2,1)S(1)} %broadcast_bitcast_fusion.2) | data formatting | bytes 16777216 | tf_op jit(solution)/shard_map/while
  173.6 7.2 %slice.25 = bf16[2,2096128]{1,0:T(2,128)(2,1)} slice(bf16[2,2097152]{1,0:T(2,128)(2,1)S(1)} %bitcast.18), slice={[0:2], [0:2096128]} | slice | bytes 16769024 | tf_op jit(solution)/shard_map/while/body/eval_jaxpr/slice | solution.py:10
  180.7 11.9 %reshape.26 = bf16[4192256]{0:T(1024)(128)(2,1)} reshape(bf16[2,2096128]{1,0:T(2,128)(2,1)} %slice.25) | data formatting | bytes 16769024 | tf_op jit(solution)/shard_map/while
  192.6 0.0 copy-start.2
  192.6 17.4 %reshape.27 = bf16[2,1024,2047]{2,1,0:T(8,128)(2,1)} reshape(bf16[4192256]{0:T(1024)(128)(2,1)} %reshape.26) | data formatting | bytes 16769024 | tf_op jit(solution)/shard_map/while/body/eval_jaxpr/reshape | solution.py:11
  210.0 0.0 copy-done.2
  210.0 3.9 %select_add_fusion.2 = f32[256,2,1024]{2,0,1:T(8,128)S(1)} fusion(f32[256,2,1024]{2,0,1:T(8,128)S(1)} %get-tuple-element.141, bf16[2,1024,2047]{2,1,0:T(8,128)(2,1)} %reshape.27, pred[]{:T(512)S(6)} %compare.4, bf16[2,256,1024]{2,1,0:T(8,128)(2,1)S(1)} %copy-done.2, s32[]{:T(128)} %get-tuple-element.140), kind=kOutput, calls=%fused_computation.3.clone.1 | convolution fusion | flops 1074790400 | bytes 8913409 | tf_op jit(solution)/shard_map/while/body/eval_jaxpr/ru,sut->rst/dot_general | solution.py:40
  213.9 2.9 copy.20
  216.8 0.0 copy-start
  216.8 0.0 copy-start.1
  216.8 0.0 all-reduce.4.cloned.1.call-update
  216.9 0.6 copy-done
  217.5 0.1 copy.16
  217.6 0.0 copy-done.1
  217.6 0.1 copy.17
  217.7 1.3 dynamic-slice
  219.6 130.8 %all-reduce.4.cloned.1.call-done = f32[256,2,1024]{2,1,0:T(2,128)} async-done(((f32[256,2,1024]{2,1,0:T(2,128)}), f32[256,2,1024]{2,1,0:T(2,128)}) %all-reduce.4.cloned.1.call-update) | async-done | bytes 2097168
  350.4 1.8 fusion.7
  (8 shorter events, 0.0 us)
Async XLA Ops:
  6.5 89.8 %all-gather.2.cloned.1.call-start = ((), (), s32[]{:S(2)}) async-start(), calls=%async_computation | async-start | bytes 1081344 | tf_op jit(solution)/shard_map/all_gather | solution.py:52
  7.3 343.1 %all-reduce.4.cloned.1.call-start = ((), (), s32[]{:S(2)}) async-start(), calls=%async_computation.1 | async-start | bytes 4194304
  133.8 17.4 %copy-start.2 = (bf16[2,256,1024]{2,1,0:T(8,128)(2,1)S(1)}, bf16[2,256,1024]{2,1,0:T(8,128)(2,1)}, u32[]{:S(2)}) copy-start(bf16[2,256,1024]{2,1,0:T(8,128)(2,1)} %get-tuple-element.149) | copy-start | bytes 3145732 | tf_op jit(solution)/shard_map/while
  192.6 17.4 %copy-start.2 = (bf16[2,256,1024]{2,1,0:T(8,128)(2,1)S(1)}, bf16[2,256,1024]{2,1,0:T(8,128)(2,1)}, u32[]{:S(2)}) copy-start(bf16[2,256,1024]{2,1,0:T(8,128)(2,1)} %get-tuple-element.149) | copy-start | bytes 3145732 | tf_op jit(solution)/shard_map/while
  216.8 0.7 copy-start
  216.8 0.8 copy-start.1
Sparse Core Ops, SparseCore 0:
  10.5 85.7 all-gather.1
  217.0 133.3 all-reduce.3
where the time goes:
time: 359 us
  waiting for transfers between devices  219 us (61%)
  local copies, waits for them, and re-layouts  115 us (32%)
  between operations  14.1 us (4%)
  matrix products  7.74 us (2%)
    unnamed x3, waiting for transfers between devices  131 us
    all_gather x1, waiting for transfers between devices, body(): lax.all_gather(panels, 'shot', axis=1, tiled=True)  87.5 us
    while x10, local copies, waits for them, and re-layouts  60.6 us
    reshape x2, local copies, waits for them, and re-layouts, toeplitz(): tiled_flat.reshape(series.shape[0], count, 2 * count - 1)[:, :, :count]  34.8 us
    slice x2, local copies, waits for them, and re-layouts, toeplitz(): tiled_flat = jnp.tile(padded, (1, count))[:, :count * (2 * count - 1)]  14.3 us
    dot_general x2, matrix products, one_point(): jnp.einsum('ru,sut->rst', panel_rows, kernel_for(point), preferred_elemen...  7.74 us
  transfers between devices with their start and end apart: 2, of which 2 were waited for; matrix products, arithmetic and copies ran while one was open for 1% of the time, Pallas kernels for 0%

commit v1 on v0

--- a/solution.py
+++ b/solution.py
@@ -2,6 +2,7 @@
 import jax.numpy as jnp
 from jax import lax
 from jax.sharding import PartitionSpec as P
+from jax.lax import all_to_all, axis_size
 
 
 def toeplitz(series):
@@ -49,7 +50,10 @@
         return convolve
 
     convolve = make_convolve(kernel_maker())
-    partial_terms = convolve(lax.all_gather(panels, "shot", axis=1, tiled=True), jnp.int32(0))
+    partial_terms = convolve(
+        jnp.concatenate(all_to_all(jnp.stack(axis_size("shot") * [panels], 0), "shot", 0, 0), 1),
+        jnp.int32(0),
+    )
     predicted = lax.psum_scatter(partial_terms, "point", scatter_dimension=0, tiled=True)
     weights = window_weights(window_lo, window_hi, traces.shape[2])
     return (weights * predicted).astype(jnp.bfloat16)

time: 359 us -> 314 us (0.87)
  waiting for transfers between devices: 219 us -> 155 us
  starting transfers between devices: 0.04 us -> 16.5 us
    all_gather x1 -> x0, waiting for transfers between devices: 87.5 us -> none  [body(): lax.all_gather(panels, 'shot', axis=1, tiled=True)]
    all_to_all x0 -> x1, waiting for transfers between devices: none -> 27.2 us  [body(): all_to_all(jnp.stack(axis_size('shot') * [panels], 0), 'shot', 0, 0)]
    all_to_all x0 -> x1, starting transfers between devices: none -> 16.5 us  [body(): all_to_all(jnp.stack(axis_size('shot') * [panels], 0), 'shot', 0, 0)]
    unnamed x3 -> x2, waiting for transfers between devices: 131 us -> 128 us
where the time goes in v1:
time: 314 us
  waiting for transfers between devices  155 us (49%)
  local copies, waits for them, and re-layouts  118 us (38%)
  starting transfers between devices  16.5 us (5%)
  between operations  14.1 us (4%)
  matrix products  7.72 us (2%)
    unnamed x2, waiting for transfers between devices  128 us
    while x10, local copies, waits for them, and re-layouts  60.6 us
    reshape x2, local copies, waits for them, and re-layouts, toeplitz(): tiled_flat.reshape(series.shape[0], count, 2 * count - 1)[:, :, :count]  34.8 us
    all_to_all x1, waiting for transfers between devices, body(): all_to_all(jnp.stack(axis_size('shot') * [panels], 0), 'shot', 0, 0)  27.2 us
    all_to_all x1, starting transfers between devices, body(): all_to_all(jnp.stack(axis_size('shot') * [panels], 0), 'shot', 0, 0)  16.5 us
    slice x2, local copies, waits for them, and re-layouts, toeplitz(): tiled_flat = jnp.tile(padded, (1, count))[:, :count * (2 * count - 1)]  14.3 us
    dot_general x2, matrix products, one_point(): jnp.einsum('ru,sut->rst', panel_rows, kernel_for(point), preferred_elemen...  7.72 us
  transfers between devices with their start and end apart: 2, of which 2 were waited for; matrix products, arithmetic and copies ran while one was open for 1% of the time, Pallas kernels for 0%

profile of v1, /device:TPU:1, one launch (start us, length us, event | category | flops | bytes accessed | tf_op | source)
XLA Modules:
  0.0 313.6 jit_solution(5359845107617854949)
XLA Ops:
  6.5 0.0 copy-start.4
  6.5 0.0 copy-start.1
  6.5 1.9 stack.2
  8.4 16.5 %all-to-all-start = ((bf16[32,2,8,1024]{3,2,1,0:T(8,128)(2,1)}), bf16[32,2,8,1024]{3,2,1,0:T(8,128)(2,1)S(1)}, u32[]{:S(2)}, u32[]{:S(2)}) async-start(bf16[32,2,8,1024]{3,2,1,0:T(8,128)(2,1)} %stack.2), calls=%async_computation | async-start | bytes 2097152 | tf_op jit(solution)/shard_map/all_to_all | solution.py:54
  24.9 0.0 all-reduce.4.cloned.1.call-start
  25.0 0.0 copy-done.4
  25.0 0.1 copy.24
  25.1 0.0 copy-done.1
  25.1 0.1 copy_multiply_fusion
  25.2 27.2 %all-to-all-done = bf16[32,2,8,1024]{3,2,1,0:T(8,128)(2,1)S(1)} async-done(((bf16[32,2,8,1024]{3,2,1,0:T(8,128)(2,1)}), bf16[32,2,8,1024]{3,2,1,0:T(8,128)(2,1)S(1)}, u32[]{:S(2)}, u32[]{:S(2)}) %all-to-all-start) | async-done | bytes 1048608 | tf_op jit(solution)/shard_map/all_to_all | solution.py:54
  52.4 1.1 copy.30
  53.5 117.5 %while.14 = (s32[]{:T(128)}, f32[256,2,1024]{2,0,1:T(8,128)S(1)}, bf16[2,256,1024]{2,1,0:T(8,128)(2,1)}, bf16[2,2,1024]{2,0,1:T(2,128)(2,1)S(1)}, s32[]{:T(128)}, /*index=5*/bf16[]{:T(256)}, s32[]{:T(128)}) while((s32[]{:T(128)}, f32[256,2,1024]{2,0,1:T(8,128)S(1)}, bf16[2,256,1024]{2,1,0:T(8,128)(2,1)}, ...), condition=%wide.region_1.2_spmd.clone, body=%wide.region_0.1_spmd.clone.sunk | while | flops 1074790400 | bytes 88609400 | solution.py:48
  53.5 1.1 broadcast_bitcast_fusion.2
  54.6 17.3 %copy.32 = bf16[1,2,1024,2048]{3,1,2,0:T(2,128)(2,1)S(1)} copy(bf16[1,2,1024,2048]{3,2,1,0:T(8,128)(2,1)S(1)} %broadcast_bitcast_fusion.2) | data formatting | bytes 16777216 | tf_op jit(solution)/shard_map/while
  71.9 7.2 %slice.25 = bf16[2,2096128]{1,0:T(2,128)(2,1)} slice(bf16[2,2097152]{1,0:T(2,128)(2,1)S(1)} %bitcast.23), slice={[0:2], [0:2096128]} | slice | bytes 16769024 | tf_op jit(solution)/shard_map/while/body/eval_jaxpr/slice | solution.py:11
  79.1 11.9 %reshape.36 = bf16[4192256]{0:T(1024)(128)(2,1)} reshape(bf16[2,2096128]{1,0:T(2,128)(2,1)} %slice.25) | data formatting | bytes 16769024 | tf_op jit(solution)/shard_map/while
  91.0 0.0 copy-start
  91.0 17.4 %reshape.37 = bf16[2,1024,2047]{2,1,0:T(8,128)(2,1)} reshape(bf16[4192256]{0:T(1024)(128)(2,1)} %reshape.36) | data formatting | bytes 16769024 | tf_op jit(solution)/shard_map/while/body/eval_jaxpr/reshape | solution.py:12
  108.4 0.0 copy-done
  108.4 3.9 %select_add_fusion.2 = f32[256,2,1024]{2,0,1:T(8,128)S(1)} fusion(f32[256,2,1024]{2,0,1:T(8,128)S(1)} %get-tuple-element.141, bf16[2,1024,2047]{2,1,0:T(8,128)(2,1)} %reshape.37, pred[]{:T(512)S(6)} %compare.4, bf16[2,256,1024]{2,1,0:T(8,128)(2,1)S(1)} %copy-done, s32[]{:T(128)} %get-tuple-element.140), kind=kOutput, calls=%fused_computation.3.clone.1 | convolution fusion | flops 1074790400 | bytes 8913409 | tf_op jit(solution)/shard_map/while/body/eval_jaxpr/ru,sut->rst/dot_general | solution.py:41
  112.3 1.1 broadcast_bitcast_fusion.2
  113.4 17.3 %copy.32 = bf16[1,2,1024,2048]{3,1,2,0:T(2,128)(2,1)S(1)} copy(bf16[1,2,1024,2048]{3,2,1,0:T(8,128)(2,1)S(1)} %broadcast_bitcast_fusion.2) | data formatting | bytes 16777216 | tf_op jit(solution)/shard_map/while
  130.7 7.2 %slice.25 = bf16[2,2096128]{1,0:T(2,128)(2,1)} slice(bf16[2,2097152]{1,0:T(2,128)(2,1)S(1)} %bitcast.23), slice={[0:2], [0:2096128]} | slice | bytes 16769024 | tf_op jit(solution)/shard_map/while/body/eval_jaxpr/slice | solution.py:11
  137.9 11.9 %reshape.36 = bf16[4192256]{0:T(1024)(128)(2,1)} reshape(bf16[2,2096128]{1,0:T(2,128)(2,1)} %slice.25) | data formatting | bytes 16769024 | tf_op jit(solution)/shard_map/while
  149.8 0.0 copy-start
  149.8 17.4 %reshape.37 = bf16[2,1024,2047]{2,1,0:T(8,128)(2,1)} reshape(bf16[4192256]{0:T(1024)(128)(2,1)} %reshape.36) | data formatting | bytes 16769024 | tf_op jit(solution)/shard_map/while/body/eval_jaxpr/reshape | solution.py:12
  167.2 0.0 copy-done
  167.2 3.9 %select_add_fusion.2 = f32[256,2,1024]{2,0,1:T(8,128)S(1)} fusion(f32[256,2,1024]{2,0,1:T(8,128)S(1)} %get-tuple-element.141, bf16[2,1024,2047]{2,1,0:T(8,128)(2,1)} %reshape.37, pred[]{:T(512)S(6)} %compare.4, bf16[2,256,1024]{2,1,0:T(8,128)(2,1)S(1)} %copy-done, s32[]{:T(128)} %get-tuple-element.140), kind=kOutput, calls=%fused_computation.3.clone.1 | convolution fusion | flops 1074790400 | bytes 8913409 | tf_op jit(solution)/shard_map/while/body/eval_jaxpr/ru,sut->rst/dot_general | solution.py:41
  171.0 2.9 copy.26
  174.0 0.0 copy-start.2
  174.0 0.0 copy-start.3
  174.0 0.0 all-reduce.4.cloned.1.call-update
  174.0 0.6 copy-done.2
  174.6 0.1 copy.21
  174.7 0.0 copy-done.3
  174.7 0.1 copy.22
  174.8 1.3 dynamic-slice
  176.8 128.2 %all-reduce.4.cloned.1.call-done = f32[256,2,1024]{2,1,0:T(2,128)} async-done(((f32[256,2,1024]{2,1,0:T(2,128)}), f32[256,2,1024]{2,1,0:T(2,128)}) %all-reduce.4.cloned.1.call-update) | async-done | bytes 2097168
  304.9 1.8 fusion.7
  (9 shorter events, 0.1 us)
Async XLA Ops:
  6.5 18.5 %copy-start.4 = (s32[2,2]{1,0:T(2,128)S(1)}, s32[2,2]{1,0:T(2,128)}, u32[]{:S(2)}) copy-start(s32[2,2]{1,0:T(2,128)} %param.9) | copy-start | bytes 52
  6.5 18.6 %copy-start.1 = (bf16[2,2,1024]{2,1,0:T(2,128)(2,1)S(1)}, bf16[2,2,1024]{2,1,0:T(2,128)(2,1)}, u32[]{:S(2)}) copy-start(bf16[2,2,1024]{2,1,0:T(2,128)(2,1)} %param.7) | copy-start | bytes 24580
  8.4 44.0 %all-to-all-start = ((bf16[32,2,8,1024]{3,2,1,0:T(8,128)(2,1)}), bf16[32,2,8,1024]{3,2,1,0:T(8,128)(2,1)S(1)}, u32[]{:S(2)}, u32[]{:S(2)}) async-start(bf16[32,2,8,1024]{3,2,1,0:T(8,128)(2,1)} %stack.2), calls=%async_computation | async-start | bytes 2097152 | tf_op jit(solution)/shard_map/all_to_all | solution.py:54
  24.9 280.0 %all-reduce.4.cloned.1.call-start = ((), (), s32[]{:S(2)}) async-start(), calls=%async_computation.1 | async-start | bytes 4194304
  91.0 17.4 %copy-start = (bf16[2,256,1024]{2,1,0:T(8,128)(2,1)S(1)}, bf16[2,256,1024]{2,1,0:T(8,128)(2,1)}, u32[]{:S(2)}) copy-start(bf16[2,256,1024]{2,1,0:T(8,128)(2,1)} %get-tuple-element.149) | copy-start | bytes 3145732 | tf_op jit(solution)/shard_map/while
  149.8 17.4 %copy-start = (bf16[2,256,1024]{2,1,0:T(8,128)(2,1)S(1)}, bf16[2,256,1024]{2,1,0:T(8,128)(2,1)}, u32[]{:S(2)}) copy-start(bf16[2,256,1024]{2,1,0:T(8,128)(2,1)} %get-tuple-element.149) | copy-start | bytes 3145732 | tf_op jit(solution)/shard_map/while
  174.0 0.7 copy-start.2
  174.0 0.8 copy-start.3
Sparse Core Ops, SparseCore 0:
  174.1 130.7 all-reduce.3
